TPU v7x, 256 devices: a whole 4x4x8 slice. The times are simulated.
256 devices in a mesh: leaf: 16 (over z, core), front: 16 (over x, y).
Axes of the slice: x: 4, y: 4, z: 8, core: 2. Of those that a mesh axis runs over, the one named last changes fastest.
Arguments:
- rhs_leaf: float32 [16, 1024, 256], P('leaf', 'front'), may hold values from -6 to 6
- rhs_top: float32 [15, 1024, 256], P(None, 'front'), may hold values from -6 to 6
- inv_leaf: bfloat16 [16, 1024, 1024], P('leaf', 'front'), as said below
- inv_top: bfloat16 [15, 1024, 1024], P(None, 'front'), as said below
- off_leaf: bfloat16 [16, 1024, 1024], P('leaf', None, 'front'), may hold values from -0.09375 to 0.09375
- off_top: bfloat16 [14, 1024, 1024], P(None, None, 'front'), may hold values from -0.09375 to 0.09375
- idx_leaf: int32 [16, 1024], P('leaf'), may hold values from 0 to 4095, as said below
- idx_top: int32 [14, 1024], replicated, may hold values from 0 to 3071, as said below
Outputs:
- leaf_solution: float32 [16, 1024, 256], P('leaf', 'front')
- ancestor_solution: float32 [16, 4, 1024, 256], P('leaf', None, 'front')
Inputs may be any that keep to these rules, and one draw needn't show every extreme that they name: `idx_leaf`: entry r of row g is a * 1024 + q with a < 4: update row r of split-level front g lands on row q of its depth-a ancestor. `idx_top`: row j belongs to the upper front with heap number h = j + 2; its entries are a * 1024 + q with a < floor(log2 h): update row r lands on row q of h's depth-a ancestor. `inv_leaf`: every block is lower triangular with a positive diagonal. `inv_top`: every block is lower triangular with a positive diagonal.
All inputs are finite; a program needn't handle non-finite values.
Results may differ from a plain program's by a relative error of at most 0.0055.
Values may be sent and summed in bfloat16 or wider, within the bound.
No kernel may reach another device: no remote copies, remote signals or barrier semaphores. Data moves between devices by JAX's collectives and lax.ppermute only.
A program may use at most 64 MiB of HBM per device.

v0:
```python
import jax
import jax.numpy as jnp
from jax import lax
from jax.sharding import PartitionSpec as P


def partner(block, axis, stride):
    count = lax.axis_size(axis)
    route = []
    for low in range(count):
        high = low | 1 << stride
        if high != low and high < count:
            route += [(low, high), (high, low)]
    return lax.ppermute(block, axis, route)


def local(rhs_leaf, rhs_top, inv_leaf, inv_top, off_leaf, off_top, idx_leaf, idx_top):
    front_width = inv_leaf.shape[2]
    rhs_count = rhs_leaf.shape[2]
    leaves = lax.axis_size("leaf")
    depth_count = leaves.bit_length() - 1
    leaf_pos = lax.axis_index("leaf")

    def apply_inverse(inverse, right_side):
        rounded = right_side.astype(jnp.bfloat16)
        return jnp.dot(
            inverse,
            lax.all_gather(rounded, "front", axis=0, tiled=True),
            preferred_element_type=jnp.float32,
        )

    def spread(off_block, solution, row_list, count):
        partial_value = jnp.dot(
            off_block, solution.astype(jnp.bfloat16), preferred_element_type=jnp.float32
        )
        dense_rows = jax.ops.segment_sum(partial_value, row_list, num_segments=count * front_width)
        dense_rows = dense_rows.reshape(count, front_width, rhs_count)
        return lax.psum_scatter(dense_rows, "front", scatter_dimension=1, tiled=True)

    leaf_solution = apply_inverse(inv_leaf[0], rhs_leaf[0])
    pending = spread(off_leaf[0], leaf_solution, idx_leaf[0], depth_count)
    solved = []
    for section_num in range(depth_count):
        pending = pending + partner(pending, "leaf", section_num)
        heap_node = jnp.right_shift(leaves + leaf_pos, section_num + 1)
        right_side = (
            lax.dynamic_index_in_dim(rhs_top, heap_node - 1, 0, keepdims=False) - pending[0]
        )
        inverse = lax.dynamic_index_in_dim(inv_top, heap_node - 1, 0, keepdims=False)
        solution = apply_inverse(inverse, right_side)
        solved.append(solution)
        if section_num + 1 < depth_count:
            off_block = lax.dynamic_index_in_dim(off_top, heap_node - 2, 0, keepdims=False)
            row_list = lax.dynamic_index_in_dim(idx_top, heap_node - 2, 0, keepdims=False)
            pending = pending[1:] + spread(
                off_block, solution, row_list, depth_count - section_num - 1
            )
    return (leaf_solution[None], jnp.stack(solved)[None])


def solution(mesh):
    placed = (
        P("leaf", "front", None),
        P(None, "front", None),
        P("leaf", "front", None),
        P(None, "front", None),
        P("leaf", None, "front"),
        P(None, None, "front"),
        P("leaf", None),
        P(),
    )
    return jax.shard_map(
        local,
        mesh=mesh,
        in_specs=placed,
        out_specs=(P("leaf", "front", None), P("leaf", None, "front", None)),
        check_vma=False,
    )
```

profile of v0, /device:TPU:32, one launch (start us, length us, event | category | flops | bytes accessed | tf_op | source)
XLA Modules:
  0.0 521.0 jit_solution(1386196292948095497)
XLA Ops:
  7.2 0.0 copy-start
  7.2 0.0 reduce-scatter.5.cloned.1.call-start
  7.2 1.0 convert_element_type.42
  8.2 24.3 %all-gather = bf16[1,1024,256]{2,1,0:T(8,128)(2,1)S(1)} all-gather(bf16[1,64,256]{2,1,0:T(8,128)(2,1)S(1)} %convert_element_type.42), channel_id=2, replica_groups=mesh['leaf'=16,'front'=16] {'front'}, dimensions={1}, use_global_device_ids=true | all-gather | bytes 557056 | tf_op jit(solution)/shard_map/all_gather | solution.py:28
  32.5 1.1 fusion.13
  33.6 0.0 copy-start.1
  33.6 1.2 convolution_bitcast_fusion
  34.8 1.3 copy.10
  36.1 8.7 %scatter_custom_fusion = f32[4096,256]{1,0:T(8,128)} fusion(s32[1024]{0:T(1024)} %bitcast.71, f32[1024,256]{1,0:T(8,128)} %copy.10, f32[]{:T(128)} %constant.69.clone.1), kind=kCustom, calls=%fused_computation.4 | custom fusion | flops 262144 | bytes 4194816 | tf_op jit(solution)/shard_map/scatter-add | solution.py:36
  44.8 0.0 copy-done.1
  44.8 0.0 reduce-scatter.5.cloned.1.call-update
  44.8 0.0 reduce-scatter.7.cloned.1.call-start
  44.9 83.3 %reduce-scatter.5.cloned.1.call-done = f32[4,64,256]{2,1,0:T(8,128)} async-done(((f32[4,1024,256]{2,1,0:T(8,128)}), f32[4,64,256]{2,1,0:T(8,128)}) %reduce-scatter.5.cloned.1.call-update) | async-done | bytes 262160 | tf_op jit(solution)/shard_map/reduce_scatter | solution.py:38
  128.2 0.0 collective-permute-start
  128.2 0.9 constant_dynamic-slice_fusion.2
  129.1 0.9 collective-permute-done
  129.9 1.0 add.98
  130.9 0.9 fusion.38
  131.8 23.3 %all-gather.1 = bf16[1,1024,256]{2,1,0:T(8,128)(2,1)S(1)} all-gather(bf16[1,64,256]{2,1,0:T(8,128)(2,1)S(1)} %fusion.38), channel_id=3, replica_groups=mesh['leaf'=16,'front'=16] {'front'}, dimensions={1}, use_global_device_ids=true | all-gather | bytes 557056 | tf_op jit(solution)/shard_map/all_gather | solution.py:28
  155.0 0.0 copy-done
  155.0 0.2 fusion.11
  155.2 1.2 fusion.23
  156.5 7.9 %scatter_custom_fusion.1 = f32[3072,256]{1,0:T(8,128)} fusion(s32[1024]{0:T(1024)S(1)} %bitcast.70, f32[1024,256]{1,0:T(8,128)S(1)} %fusion.23, f32[]{:T(128)} %constant.69.clone.1), kind=kCustom, calls=%fused_computation.6 | custom fusion | flops 262144 | bytes 3145732 | tf_op jit(solution)/shard_map/scatter-add | solution.py:36
  164.4 0.0 reduce-scatter.7.cloned.1.call-update
  164.4 0.0 reduce-scatter.9.cloned.1.call-start
  164.4 79.7 %reduce-scatter.7.cloned.1.call-done = f32[3,64,256]{2,1,0:T(8,128)} async-done(((f32[3,1024,256]{2,1,0:T(8,128)}), f32[3,64,256]{2,1,0:T(8,128)}) %reduce-scatter.7.cloned.1.call-update) | async-done | bytes 196624 | tf_op jit(solution)/shard_map/reduce_scatter | solution.py:38
  244.1 0.9 slice_add_fusion
  245.1 0.6 collective-permute-start.1
  245.6 5.2 collective-permute-done.1
  250.9 0.9 fusion.37
  251.7 23.5 %all-gather.2 = bf16[1,1024,256]{2,1,0:T(8,128)(2,1)S(1)} all-gather(bf16[1,64,256]{2,1,0:T(8,128)(2,1)S(1)} %fusion.37), channel_id=4, replica_groups=mesh['leaf'=16,'front'=16] {'front'}, dimensions={1}, use_global_device_ids=true | all-gather | bytes 557056 | tf_op jit(solution)/shard_map/all_gather | solution.py:28
  275.2 0.2 fusion.9
  275.4 1.2 fusion.20
  276.7 7.5 %scatter_custom_fusion.2 = f32[2048,256]{1,0:T(8,128)} fusion(s32[1024]{0:T(1024)S(1)} %bitcast.69, f32[1024,256]{1,0:T(8,128)S(1)} %fusion.20, f32[]{:T(128)} %constant.69.clone.1), kind=kCustom, calls=%fused_computation.10 | custom fusion | flops 262144 | bytes 2097156 | tf_op jit(solution)/shard_map/scatter-add | solution.py:36
  284.1 0.0 reduce-scatter.9.cloned.1.call-update
  284.2 0.0 reduce-scatter.11.cloned.1.call-start
  284.2 78.2 %reduce-scatter.9.cloned.1.call-done = f32[2,64,256]{2,1,0:T(8,128)} async-done(((f32[2,1024,256]{2,1,0:T(8,128)}), f32[2,64,256]{2,1,0:T(8,128)}) %reduce-scatter.9.cloned.1.call-update) | async-done | bytes 131088 | tf_op jit(solution)/shard_map/reduce_scatter | solution.py:38
  362.4 0.9 slice_add_fusion.1
  363.3 2.6 collective-permute-start.2
  365.9 3.8 collective-permute-done.2
  369.8 0.9 fusion.36
  370.6 23.2 %all-gather.3 = bf16[1,1024,256]{2,1,0:T(8,128)(2,1)S(1)} all-gather(bf16[1,64,256]{2,1,0:T(8,128)(2,1)S(1)} %fusion.36), channel_id=5, replica_groups=mesh['leaf'=16,'front'=16] {'front'}, dimensions={1}, use_global_device_ids=true | all-gather | bytes 557056 | tf_op jit(solution)/shard_map/all_gather | solution.py:28
  393.9 0.2 fusion.7
  394.1 1.2 fusion.17
  395.3 7.1 %scatter_custom_fusion.3 = f32[1024,256]{1,0:T(8,128)} fusion(s32[1024]{0:T(1024)S(1)} %bitcast.68, f32[1024,256]{1,0:T(8,128)S(1)} %fusion.17, f32[]{:T(128)} %constant.69.clone.1), kind=kCustom, calls=%fused_computation.21 | custom fusion | flops 262144 | bytes 1048580 | tf_op jit(solution)/shard_map/scatter-add | solution.py:36
  402.4 0.0 reduce-scatter.11.cloned.1.call-update
  402.4 77.7 %reduce-scatter.11.cloned.1.call-done = f32[1,64,256]{2,1,0:T(8,128)} async-done(((f32[1,1024,256]{2,1,0:T(8,128)}), f32[1,64,256]{2,1,0:T(8,128)}) %reduce-scatter.11.cloned.1.call-update) | async-done | bytes 65552 | tf_op jit(solution)/shard_map/reduce_scatter | solution.py:38
  480.1 0.8 slice_add_fusion.2
  480.9 5.0 collective-permute-start.3
  485.9 3.4 collective-permute-done.3
  489.3 0.9 subtract_convert_fusion
  490.2 23.3 %all-gather.4 = bf16[1,1024,256]{2,1,0:T(8,128)(2,1)S(1)} all-gather(bf16[1,64,256]{2,1,0:T(8,128)(2,1)S(1)} %subtract_convert_fusion), channel_id=6, replica_groups=mesh['leaf'=16,'front'=16] {'front'}, dimensions={1}, use_global_device_ids=true | all-gather | bytes 557056 | tf_op jit(solution)/shard_map/all_gather | solution.py:28
  513.5 0.2 convolution_bitcast_fusion.1
  513.7 0.7 maximum_bitcast_fusion
  (2 shorter events, 0.0 us)
Async XLA Ops:
  7.2 147.9 %copy-start = (bf16[15,64,1024]{2,1,0:T(8,128)(2,1)S(1)}, bf16[15,64,1024]{2,1,0:T(8,128)(2,1)}, u32[]{:S(2)}) copy-start(bf16[15,64,1024]{2,1,0:T(8,128)(2,1)} %param.11) | copy-start | bytes 5898244
  7.2 121.0 %reduce-scatter.5.cloned.1.call-start = ((), (), s32[]{:S(2)}) async-start(), calls=%async_computation.4 | async-start | bytes 4456448 | tf_op jit(solution)/shard_map/reduce_scatter | solution.py:38
  33.6 11.2 %copy-start.1 = (f32[64,256]{1,0:T(8,128)}, f32[64,256]{1,0:T(8,128)S(1)}, u32[]{:S(2)}) copy-start(f32[64,256]{1,0:T(8,128)S(1)} %fusion.13) | copy-start | bytes 196612
  44.8 199.3 %reduce-scatter.7.cloned.1.call-start = ((), (), s32[]{:S(2)}) async-start(), calls=%async_computation.5 | async-start | bytes 3342336 | tf_op jit(solution)/shard_map/reduce_scatter | solution.py:38
  128.2 1.7 collective-permute-start
  164.4 198.0 %reduce-scatter.9.cloned.1.call-start = ((), (), s32[]{:S(2)}) async-start(), calls=%async_computation.6 | async-start | bytes 2228224 | tf_op jit(solution)/shard_map/reduce_scatter | solution.py:38
  245.1 5.8 %collective-permute-start.1 = (f32[3,64,256]{2,1,0:T(8,128)S(1)}, f32[3,64,256]{2,1,0:T(8,128)S(1)}, u32[]{:S(2)}, u32[]{:S(2)}) collective-permute-start(f32[3,64,256]{2,1,0:T(8,128)S(1)} %slice_add_fusion), channel_id=1, source_target_pairs={{0,32},{32,0},{16,48},{48,16},{64,96},{96,64},{80,112},{112,80},{1... | collective-permute-start | bytes 589832 | tf_op jit(solution)/shard_map/ppermute | solution.py:14
  284.2 195.9 %reduce-scatter.11.cloned.1.call-start = ((), (), s32[]{:S(2)}) async-start(), calls=%async_computation.7 | async-start | bytes 1114112 | tf_op jit(solution)/shard_map/reduce_scatter | solution.py:38
  363.3 6.5 %collective-permute-start.2 = (f32[2,64,256]{2,1,0:T(8,128)S(1)}, f32[2,64,256]{2,1,0:T(8,128)S(1)}, u32[]{:S(2)}, u32[]{:S(2)}) collective-permute-start(f32[2,64,256]{2,1,0:T(8,128)S(1)} %slice_add_fusion.1), channel_id=1, source_target_pairs={{0,64},{64,0},{16,80},{80,16},{32,96},{96,32},{48,112},{112,48},{1... | collective-permute-start | bytes 393224 | tf_op jit(solution)/shard_map/ppermute | solution.py:14
  480.9 8.4 %collective-permute-start.3 = (f32[1,64,256]{2,1,0:T(8,128)S(1)}, f32[1,64,256]{2,1,0:T(8,128)S(1)}, u32[]{:S(2)}, u32[]{:S(2)}) collective-permute-start(f32[1,64,256]{2,1,0:T(8,128)S(1)} %slice_add_fusion.2), channel_id=1, source_target_pairs={{0,128},{128,0},{16,144},{144,16},{32,160},{160,32},{48,176},{176,... | collective-permute-start | bytes 196616 | tf_op jit(solution)/shard_map/ppermute | solution.py:14
Sparse Core Ops, SparseCore 0:
  45.0 83.1 reduce-scatter.4
  164.5 79.5 reduce-scatter.6
  284.3 78.0 reduce-scatter.8
  402.5 77.5 reduce-scatter.10
where the time goes:
time: 522 us; the launch traced here: 521 us
  waiting for transfers between devices  332 us (64%)
  blocking collectives  118 us (23%)
  other arithmetic  39.9 us (8%)
  between operations  13.9 us (3%)
  starting transfers between devices  8.32 us (2%)
  matrix products  6.91 us (1%)
    reduce_scatter x4, waiting for transfers between devices, spread(): lax.psum_scatter(dense_rows, 'front', scatter_dimension=1, tiled=True)  319 us
    all_gather x5, blocking collectives, apply_inverse(): lax.all_gather(rounded, 'front', axis=0, tiled=True)  118 us
    scatter-add x4, other arithmetic, spread(): jax.ops.segment_sum(partial_value, row_list, num_segments=count * front_w...  31.1 us
    ppermute x4, waiting for transfers between devices, partner(): return lax.ppermute(block, axis, route)  13.3 us
  transfers between devices with their start and end apart: 8, of which 8 were waited for; matrix products, arithmetic and copies ran while one was open for 0% of the time, Pallas kernels for 0%

commit v1 on v0

--- a/solution.py
+++ b/solution.py
@@ -22,12 +22,16 @@
     leaf_pos = lax.axis_index("leaf")
 
     def apply_inverse(inverse, right_side):
+
+        def lift_task(shard_in, axis_key):
+            z1 = lax.axis_size(axis_key)
+            before = jnp.stack([shard_in] * z1)
+            t_next = lax.all_to_all(before, axis_key, 0, 0)
+            all_values = jnp.concatenate(t_next, axis=0)
+            return all_values
+
         rounded = right_side.astype(jnp.bfloat16)
-        return jnp.dot(
-            inverse,
-            lax.all_gather(rounded, "front", axis=0, tiled=True),
-            preferred_element_type=jnp.float32,
-        )
+        return jnp.dot(inverse, lift_task(rounded, "front"), preferred_element_type=jnp.float32)
 
     def spread(off_block, solution, row_list, count):
         partial_value = jnp.dot(

time: 522 us -> 480 us (0.920)
  blocking collectives: 118 us -> 62.6 us
  waiting for transfers between devices: 332 us -> 340 us
    all_gather x5 -> x0, blocking collectives: 118 us -> none  [apply_inverse(): lax.all_gather(rounded, 'front', axis=0, tiled=True)]
    all_to_all x0 -> x4, blocking collectives: none -> 62.6 us  [lift_task(): t_next = lax.all_to_all(before, axis_key, 0, 0)]
    all_to_all x0 -> x1, waiting for transfers between devices: none -> 10.8 us  [lift_task(): t_next = lax.all_to_all(before, axis_key, 0, 0)]
  transfers between devices with their start and end apart: 8 -> 9, of which waited for: 8 -> 9; matrix products, arithmetic and copies ran while one was open for 0% -> 0% of each run, Pallas kernels for 0% -> 0%
where the time goes in v1:
time: 480 us; the launch traced here: 479 us
  waiting for transfers between devices  340 us (71%)
  blocking collectives  62.6 us (13%)
  other arithmetic  39.9 us (8%)
  between operations  13.9 us (3%)
  starting transfers between devices  13.1 us (3%)
  matrix products  5.97 us (1%)
    reduce_scatter x4, waiting for transfers between devices, spread(): lax.psum_scatter(dense_rows, 'front', scatter_dimension=1, tiled=True)  315 us
    all_to_all x4, blocking collectives, lift_task(): t_next = lax.all_to_all(before, axis_key, 0, 0)  62.6 us
    scatter-add x4, other arithmetic, spread(): jax.ops.segment_sum(partial_value, row_list, num_segments=count * front_w...  31.1 us
    ppermute x4, waiting for transfers between devices, partner(): return lax.ppermute(block, axis, route)  14.2 us
    all_to_all x1, waiting for transfers between devices, lift_task(): t_next = lax.all_to_all(before, axis_key, 0, 0)  10.8 us
  transfers between devices with their start and end apart: 9, of which 9 were waited for; matrix products, arithmetic and copies ran while one was open for 0% of the time, Pallas kernels for 0%

profile of v1, /device:TPU:32, one launch (start us, length us, event | category | flops | bytes accessed | tf_op | source)
XLA Modules:
  0.0 479.2 jit_solution(2332712241670819883)
XLA Ops:
  7.2 0.0 copy-start
  7.2 0.0 copy-start.2
  7.2 0.0 reduce-scatter.5.cloned.1.call-start
  7.2 1.0 convert_bitcast_fusion
  8.3 18.3 %all_to_all.25 = bf16[16,64,256]{2,1,0:T(8,128)(2,1)S(1)} all-to-all(bf16[16,64,256]{2,1,0:T(8,128)(2,1)S(1)} %stack.31), channel_id=1, replica_groups=mesh['leaf'=16,'front'=16] {'front'}, dimensions={0} | all-to-all | bytes 1048576 | tf_op jit(solution)/shard_map/all_to_all | solution.py:29
  26.6 1.1 fusion.22
  27.7 0.0 copy-done.2
  27.7 0.0 copy-start.1
  27.7 0.3 convolution_bitcast_fusion
  28.1 1.3 copy.10
  29.4 8.7 %scatter_custom_fusion = f32[4096,256]{1,0:T(8,128)} fusion(s32[1024]{0:T(1024)} %bitcast.81, f32[1024,256]{1,0:T(8,128)} %copy.10, f32[]{:T(128)} %constant.69.clone.1), kind=kCustom, calls=%fused_computation.4 | custom fusion | flops 262144 | bytes 4194816 | tf_op jit(solution)/shard_map/scatter-add | solution.py:40
  38.1 0.0 copy-done.1
  38.1 0.0 reduce-scatter.5.cloned.1.call-update
  38.1 81.9 %reduce-scatter.5.cloned.1.call-done = f32[4,64,256]{2,1,0:T(8,128)} async-done(((f32[4,1024,256]{2,1,0:T(8,128)}), f32[4,64,256]{2,1,0:T(8,128)}) %reduce-scatter.5.cloned.1.call-update) | async-done | bytes 262160 | tf_op jit(solution)/shard_map/reduce_scatter | solution.py:42
  120.0 0.0 collective-permute-start
  120.0 1.7 collective-permute-done
  121.8 1.0 add.98
  122.7 0.9 fusion.35
  123.6 0.8 stack.33
  124.4 4.9 %all-to-all-start.1 = ((bf16[16,64,256]{2,1,0:T(8,128)(2,1)}), bf16[16,64,256]{2,1,0:T(8,128)(2,1)S(1)}, u32[]{:S(2)}, u32[]{:S(2)}) async-start(bf16[16,64,256]{2,1,0:T(8,128)(2,1)} %stack.33), calls=%async_computation.2 | async-start | bytes 1048576 | tf_op jit(solution)/shard_map/all_to_all | solution.py:29
  129.3 0.0 reduce-scatter.7.cloned.1.call-start
  129.4 0.9 constant_dynamic-slice_fusion.2
  130.3 10.8 %all-to-all-done.1 = bf16[16,64,256]{2,1,0:T(8,128)(2,1)S(1)} async-done(((bf16[16,64,256]{2,1,0:T(8,128)(2,1)}), bf16[16,64,256]{2,1,0:T(8,128)(2,1)S(1)}, u32[]{:S(2)}, u32[]{:S(2)}) %all-to-all-start.1) | async-done | bytes 524320 | tf_op jit(solution)/shard_map/all_to_all | solution.py:29
  141.1 0.0 copy-done
  141.1 0.2 fusion.20
  141.3 1.2 fusion.15
  142.6 7.9 %scatter_custom_fusion.1 = f32[3072,256]{1,0:T(8,128)} fusion(s32[1024]{0:T(1024)S(1)} %bitcast.80, f32[1024,256]{1,0:T(8,128)S(1)} %fusion.15, f32[]{:T(128)} %constant.69.clone.1), kind=kCustom, calls=%fused_computation.6 | custom fusion | flops 262144 | bytes 3145732 | tf_op jit(solution)/shard_map/scatter-add | solution.py:40
  150.5 0.0 reduce-scatter.7.cloned.1.call-update
  150.5 0.0 reduce-scatter.9.cloned.1.call-start
  150.5 78.9 %reduce-scatter.7.cloned.1.call-done = f32[3,64,256]{2,1,0:T(8,128)} async-done(((f32[3,1024,256]{2,1,0:T(8,128)}), f32[3,64,256]{2,1,0:T(8,128)}) %reduce-scatter.7.cloned.1.call-update) | async-done | bytes 196624 | tf_op jit(solution)/shard_map/reduce_scatter | solution.py:42
  229.5 0.9 slice_add_fusion
  230.4 0.6 collective-permute-start.1
  231.0 5.2 %collective-permute-done.1 = f32[3,64,256]{2,1,0:T(8,128)S(1)} collective-permute-done((f32[3,64,256]{2,1,0:T(8,128)S(1)}, f32[3,64,256]{2,1,0:T(8,128)S(1)}, u32[]{:S(2)}, u32[]{:S(2)}) %collective-permute-start.1) | collective-permute-done | bytes 196640 | tf_op jit(solution)/shard_map/ppermute | solution.py:14
  236.2 0.9 fusion.36
  237.1 14.7 %all_to_all.26 = bf16[16,64,256]{2,1,0:T(8,128)(2,1)S(1)} all-to-all(bf16[16,64,256]{2,1,0:T(8,128)(2,1)S(1)} %stack.36), channel_id=1, replica_groups=mesh['leaf'=16,'front'=16] {'front'}, dimensions={0} | all-to-all | bytes 1048576 | tf_op jit(solution)/shard_map/all_to_all | solution.py:29
  251.9 0.2 fusion.17
  252.1 1.2 fusion.11
  253.3 7.5 %scatter_custom_fusion.2 = f32[2048,256]{1,0:T(8,128)} fusion(s32[1024]{0:T(1024)S(1)} %bitcast.79, f32[1024,256]{1,0:T(8,128)S(1)} %fusion.11, f32[]{:T(128)} %constant.69.clone.1), kind=kCustom, calls=%fused_computation.10 | custom fusion | flops 262144 | bytes 2097156 | tf_op jit(solution)/shard_map/scatter-add | solution.py:40
  260.8 0.0 reduce-scatter.9.cloned.1.call-update
  260.8 0.0 reduce-scatter.11.cloned.1.call-start
  260.9 77.4 %reduce-scatter.9.cloned.1.call-done = f32[2,64,256]{2,1,0:T(8,128)} async-done(((f32[2,1024,256]{2,1,0:T(8,128)}), f32[2,64,256]{2,1,0:T(8,128)}) %reduce-scatter.9.cloned.1.call-update) | async-done | bytes 131088 | tf_op jit(solution)/shard_map/reduce_scatter | solution.py:42
  338.3 0.9 slice_add_fusion.1
  339.2 2.6 collective-permute-start.2
  341.8 3.8 collective-permute-done.2
  345.6 0.9 fusion.37
  346.6 14.7 %all_to_all.27 = bf16[16,64,256]{2,1,0:T(8,128)(2,1)S(1)} all-to-all(bf16[16,64,256]{2,1,0:T(8,128)(2,1)S(1)} %stack.39), channel_id=1, replica_groups=mesh['leaf'=16,'front'=16] {'front'}, dimensions={0} | all-to-all | bytes 1048576 | tf_op jit(solution)/shard_map/all_to_all | solution.py:29
  361.3 0.2 fusion.13
  361.5 1.2 fusion.8
  362.7 7.1 %scatter_custom_fusion.3 = f32[1024,256]{1,0:T(8,128)} fusion(s32[1024]{0:T(1024)S(1)} %bitcast.78, f32[1024,256]{1,0:T(8,128)S(1)} %fusion.8, f32[]{:T(128)} %constant.69.clone.1), kind=kCustom, calls=%fused_computation.12 | custom fusion | flops 262144 | bytes 1048580 | tf_op jit(solution)/shard_map/scatter-add | solution.py:40
  369.8 0.0 reduce-scatter.11.cloned.1.call-update
  369.8 76.9 %reduce-scatter.11.cloned.1.call-done = f32[1,64,256]{2,1,0:T(8,128)} async-done(((f32[1,1024,256]{2,1,0:T(8,128)}), f32[1,64,256]{2,1,0:T(8,128)}) %reduce-scatter.11.cloned.1.call-update) | async-done | bytes 65552 | tf_op jit(solution)/shard_map/reduce_scatter | solution.py:42
  446.8 0.8 slice_add_fusion.2
  447.6 4.9 %collective-permute-start.3 = (f32[1,64,256]{2,1,0:T(8,128)S(1)}, f32[1,64,256]{2,1,0:T(8,128)S(1)}, u32[]{:S(2)}, u32[]{:S(2)}) collective-permute-start(f32[1,64,256]{2,1,0:T(8,128)S(1)} %slice_add_fusion.2), channel_id=1, source_target_pairs={{0,128},{128,0},{16,144},{144,16},{32,160},{160,32},{48,176},{176,... | collective-permute-start | bytes 196616 | tf_op jit(solution)/shard_map/ppermute | solution.py:14
  452.5 3.5 collective-permute-done.3
  456.0 0.9 fusion.34
  456.9 14.8 %all_to_all.28 = bf16[16,64,256]{2,1,0:T(8,128)(2,1)S(1)} all-to-all(bf16[16,64,256]{2,1,0:T(8,128)(2,1)S(1)} %stack.42), channel_id=1, replica_groups=mesh['leaf'=16,'front'=16] {'front'}, dimensions={0} | all-to-all | bytes 1048576 | tf_op jit(solution)/shard_map/all_to_all | solution.py:29
  471.7 0.2 convolution_bitcast_fusion.1
  471.9 0.7 maximum_bitcast_fusion
  (6 shorter events, 0.2 us)
Async XLA Ops:
  7.2 134.0 %copy-start = (bf16[15,64,1024]{2,1,0:T(8,128)(2,1)S(1)}, bf16[15,64,1024]{2,1,0:T(8,128)(2,1)}, u32[]{:S(2)}) copy-start(bf16[15,64,1024]{2,1,0:T(8,128)(2,1)} %param.11) | copy-start | bytes 5898244
  7.2 20.5 %copy-start.2 = (bf16[1,1024,64]{1,2,0:T(8,128)(2,1)S(1)}, bf16[1,1024,64]{1,2,0:T(8,128)(2,1)}, u32[]{:S(2)}) copy-start(bf16[1,1024,64]{1,2,0:T(8,128)(2,1)} %param.12) | copy-start | bytes 393220
  7.2 112.8 %reduce-scatter.5.cloned.1.call-start = ((), (), s32[]{:S(2)}) async-start(), calls=%async_computation.9 | async-start | bytes 4456448 | tf_op jit(solution)/shard_map/reduce_scatter | solution.py:42
  27.7 10.3 %copy-start.1 = (f32[64,256]{1,0:T(8,128)}, f32[64,256]{1,0:T(8,128)S(1)}, u32[]{:S(2)}) copy-start(f32[64,256]{1,0:T(8,128)S(1)} %fusion.22) | copy-start | bytes 196612
  120.0 1.7 collective-permute-start
  124.4 16.7 %all-to-all-start.1 = ((bf16[16,64,256]{2,1,0:T(8,128)(2,1)}), bf16[16,64,256]{2,1,0:T(8,128)(2,1)S(1)}, u32[]{:S(2)}, u32[]{:S(2)}) async-start(bf16[16,64,256]{2,1,0:T(8,128)(2,1)} %stack.33), calls=%async_computation.2 | async-start | bytes 1048576 | tf_op jit(solution)/shard_map/all_to_all | solution.py:29
  129.3 100.1 %reduce-scatter.7.cloned.1.call-start = ((), (), s32[]{:S(2)}) async-start(), calls=%async_computation.10 | async-start | bytes 3342336 | tf_op jit(solution)/shard_map/reduce_scatter | solution.py:42
  150.5 187.8 %reduce-scatter.9.cloned.1.call-start = ((), (), s32[]{:S(2)}) async-start(), calls=%async_computation.11 | async-start | bytes 2228224 | tf_op jit(solution)/shard_map/reduce_scatter | solution.py:42
  230.4 5.8 %collective-permute-start.1 = (f32[3,64,256]{2,1,0:T(8,128)S(1)}, f32[3,64,256]{2,1,0:T(8,128)S(1)}, u32[]{:S(2)}, u32[]{:S(2)}) collective-permute-start(f32[3,64,256]{2,1,0:T(8,128)S(1)} %slice_add_fusion), channel_id=1, source_target_pairs={{0,32},{32,0},{16,48},{48,16},{64,96},{96,64},{80,112},{112,80},{1... | collective-permute-start | bytes 589832 | tf_op jit(solution)/shard_map/ppermute | solution.py:14
  260.8 185.9 %reduce-scatter.11.cloned.1.call-start = ((), (), s32[]{:S(2)}) async-start(), calls=%async_computation.12 | async-start | bytes 1114112 | tf_op jit(solution)/shard_map/reduce_scatter | solution.py:42
  339.2 6.4 %collective-permute-start.2 = (f32[2,64,256]{2,1,0:T(8,128)S(1)}, f32[2,64,256]{2,1,0:T(8,128)S(1)}, u32[]{:S(2)}, u32[]{:S(2)}) collective-permute-start(f32[2,64,256]{2,1,0:T(8,128)S(1)} %slice_add_fusion.1), channel_id=1, source_target_pairs={{0,64},{64,0},{16,80},{80,16},{32,96},{96,32},{48,112},{112,48},{1... | collective-permute-start | bytes 393224 | tf_op jit(solution)/shard_map/ppermute | solution.py:14
  447.6 8.4 %collective-permute-start.3 = (f32[1,64,256]{2,1,0:T(8,128)S(1)}, f32[1,64,256]{2,1,0:T(8,128)S(1)}, u32[]{:S(2)}, u32[]{:S(2)}) collective-permute-start(f32[1,64,256]{2,1,0:T(8,128)S(1)} %slice_add_fusion.2), channel_id=1, source_target_pairs={{0,128},{128,0},{16,144},{144,16},{32,160},{160,32},{48,176},{176,... | collective-permute-start | bytes 196616 | tf_op jit(solution)/shard_map/ppermute | solution.py:14
Sparse Core Ops, SparseCore 0:
  38.2 81.7 reduce-scatter.4
  150.6 78.8 reduce-scatter.6
  260.9 77.2 reduce-scatter.8
  369.9 76.7 reduce-scatter.10
